TPU v7x, 32 devices: a whole 2x2x4 slice. The times are simulated.
32 devices in a mesh: blk: 8 (over z, y), tp: 4 (over x, core).
Axes of the slice: x: 2, y: 2, z: 4, core: 2. Of those that a mesh axis runs over, the one named last changes fastest.
Arguments:
- tokens: bfloat16 [4096, 1664], P('blk', 'tp'), may hold values from -8 to 8
- block_split: int32 [16], replicated, may hold values from 0 to 15, each once
- req_lengths: int32 [32], replicated, may hold values from 1 to 125, as said below
- req_owners: int32 [32], replicated, may hold values from 0 to 7, as said below
- norm1_gain: float32 [1664], replicated, may hold values from 0.25 to 1.75
- qkv_weight: bfloat16 [1664, 3, 1664], P(None, None, 'tp'), may hold values from -2 to 2
- out_weight: bfloat16 [1664, 1664], P('tp'), may hold values from -0.15625 to 0.15625
- norm2_gain: float32 [1664], replicated, may hold values from 0.25 to 1.75
- up_weight: bfloat16 [1664, 8192], P(None, 'tp'), may hold values from -0.15625 to 0.15625
- down_weight: bfloat16 [8192, 1664], P('tp'), may hold values from -0.0625 to 0.0625
- merge_gain: float32 [1664], replicated, may hold values from 0.25 to 1.75
- merge_weight: bfloat16 [6656, 1664], P(None, 'tp'), may hold values from -0.078125 to 0.078125
Outputs:
- returned: bfloat16 [1024, 1664], P('blk', 'tp')
Inputs may be any that keep to these rules, and one draw needn't show every extreme that they name: Index d of blk holds packed blocks block_split[2d] and block_split[2d + 1], each of 256 tokens; every block once. `req_lengths`: lengths count merge groups of 4 tokens; the requests of each owner add up to exactly 128 groups. `req_owners`: every owner index holds exactly 4 requests.
All inputs are finite; a program needn't handle non-finite values.
Results may differ from a plain program's by a relative error of at most 0.015.
Values may be sent and summed in bfloat16 or wider, within the bound.
A program may use at most 128 MiB of HBM per device.

v0:
```python
import math

import jax
import jax.numpy as jnp
from jax import lax
from jax.sharding import PartitionSpec as P

HDIM = 104


EPSILON = 1e-06
MASKED = -1e30


def layer_norm(values, norm_gain):
    values = values.astype(jnp.float32)
    row_mean = jnp.mean(values, axis=-1, keepdims=True)
    centred = values - row_mean
    spread = jnp.mean(centred * centred, axis=-1, keepdims=True)
    return centred * lax.rsqrt(spread + EPSILON) * norm_gain


def request_tables(req_lengths, req_owners):
    request_ends = jnp.cumsum(req_lengths)
    starts = request_ends - req_lengths
    position = jnp.arange(req_lengths.shape[0], dtype=jnp.int32)
    earlier = (req_owners[None, :] == req_owners[:, None]) & (position[None, :] < position[:, None])
    owner_offset = jnp.sum(jnp.where(earlier, req_lengths[None, :], 0), axis=1)
    return (starts, request_ends, owner_offset)


def segment_of(row_ids, block_split, request_ends, half_rows):
    slot_index = row_ids // half_rows
    places = jnp.arange(block_split.shape[0], dtype=jnp.int32)
    packed_block = jnp.sum(
        jnp.where(slot_index[:, None] == places[None, :], block_split[None, :], 0), axis=1
    )
    group_index = (packed_block * half_rows + row_ids % half_rows) // 4
    return jnp.sum((request_ends[None, :] <= group_index[:, None]).astype(jnp.int32), axis=1)


def owner_groups(
    owner, req_lengths, req_owners, block_split, starts, owner_offset, slot_count, half_groups
):
    slots = jnp.arange(slot_count, dtype=jnp.int32)
    chosen = (
        (req_owners[None, :] == owner)
        & (owner_offset[None, :] <= slots[:, None])
        & (slots[:, None] < (owner_offset + req_lengths)[None, :])
    )
    packed = jnp.sum(jnp.where(chosen, (starts - owner_offset)[None, :], 0), axis=1) + slots
    request = jnp.sum(
        jnp.where(chosen, jnp.arange(req_lengths.shape[0], dtype=jnp.int32)[None, :], 0), axis=1
    )
    packed_block = packed // half_groups
    places = jnp.arange(block_split.shape[0], dtype=jnp.int32)
    held_at = jnp.sum(
        jnp.where(block_split[None, :] == packed_block[:, None], places[None, :], 0), axis=1
    )
    return (held_at * half_groups + packed % half_groups, request)


def attend(carried, query_rows, query_seg, key_rows, value_rows, key_seg):
    maxima, totals, accumulated = carried
    query_count = query_rows.shape[0]
    key_count = key_rows.shape[0]
    head_count = accumulated.shape[1]
    head_size = accumulated.shape[2]
    query_heads = query_rows.reshape(query_count, head_count, head_size)
    key_heads = key_rows.reshape(key_count, head_count, head_size)
    value_heads = value_rows.reshape(key_count, head_count, head_size)
    scores = jnp.einsum(
        "qhd,khd->hqk", query_heads, key_heads, preferred_element_type=jnp.float32
    ) * head_size ** (-0.5)
    same_request = (query_seg[:, None] == key_seg[None, :])[None, :, :]
    scores = jnp.where(same_request, scores, MASKED)
    new_max = jnp.maximum(maxima, jnp.max(scores, axis=2))
    weights = jnp.where(same_request, jnp.exp(scores - new_max[:, :, None]), 0.0)
    factor = jnp.exp(maxima - new_max)
    totals = totals * factor + jnp.sum(weights, axis=2)
    mixed_values = jnp.einsum(
        "hqk,khd->qhd",
        weights.astype(jnp.bfloat16),
        value_heads,
        preferred_element_type=jnp.float32,
    )
    accumulated = accumulated * jnp.transpose(factor)[:, :, None] + mixed_values
    return (new_max, totals, accumulated)


def pick_rows(targets, carried, received):
    inside = (targets >= 0) & (targets < received.shape[0])
    picked = jnp.take(received, jnp.clip(targets, 0, received.shape[0] - 1), axis=0)
    return jnp.where(inside[:, None], picked, carried)


def body(
    tokens,
    block_split,
    req_lengths,
    req_owners,
    norm1_gain,
    qkv_weight,
    out_weight,
    norm2_gain,
    up_weight,
    down_weight,
    merge_gain,
    merge_weight,
):
    tok_rows = tokens.shape[0]
    half_rows = tok_rows // 2
    group_rows = tok_rows // 4
    my_index = lax.axis_index("blk")
    starts, request_ends, owner_offset = request_tables(req_lengths, req_owners)
    merged_targets, request = owner_groups(
        my_index,
        req_lengths,
        req_owners,
        block_split,
        starts,
        owner_offset,
        group_rows,
        half_rows // 4,
    )
    query_seg = segment_of(
        my_index * tok_rows + jnp.arange(tok_rows, dtype=jnp.int32),
        block_split,
        request_ends,
        half_rows,
    )
    features = lax.all_gather(tokens, "tp", axis=1, tiled=True)
    normed1 = layer_norm(features, norm1_gain).astype(jnp.bfloat16)
    projected = jnp.einsum(
        "td,dcf->ctf", normed1, qkv_weight, preferred_element_type=jnp.float32
    ).astype(jnp.bfloat16)
    queries = projected[0]
    head_count = qkv_weight.shape[2] // HDIM
    start_state = (
        jnp.full((head_count, tok_rows), MASKED, jnp.float32),
        jnp.zeros((head_count, tok_rows), jnp.float32),
        jnp.zeros((tok_rows, head_count, HDIM), jnp.float32),
    )
    carried = start_state
    key_piece = lax.all_gather(projected[1], "blk", axis=0, tiled=True)
    value_piece = lax.all_gather(projected[2], "blk", axis=0, tiled=True)
    key_count = key_piece.shape[0]
    block_rows = math.gcd(key_count, tok_rows * max(1, 1024 // tok_rows))
    key_seg = segment_of(
        jnp.arange(key_count, dtype=jnp.int32), block_split, request_ends, half_rows
    )
    stacked = (
        key_piece.reshape(key_count // block_rows, block_rows, -1),
        value_piece.reshape(key_count // block_rows, block_rows, -1),
        key_seg.reshape(key_count // block_rows, block_rows),
    )

    def visit_block(running, block_item):
        key_rows, value_rows, seg_rows = block_item
        touches = jnp.any(query_seg[:, None] == seg_rows[None, :])
        running = lax.cond(
            touches,
            lambda kept: attend(kept, queries, query_seg, key_rows, value_rows, seg_rows),
            lambda kept: kept,
            running,
        )
        return (running, None)

    carried, unused = lax.scan(visit_block, carried, stacked)
    running = carried
    maxima, totals, accumulated = running
    attended = (
        (accumulated / jnp.transpose(totals)[:, :, None]).reshape(tok_rows, -1).astype(jnp.bfloat16)
    )
    residual = features.astype(jnp.float32)
    after_attention = residual + lax.psum(
        jnp.dot(attended, out_weight, preferred_element_type=jnp.float32).astype(jnp.bfloat16), "tp"
    ).astype(jnp.float32)
    normed2 = layer_norm(after_attention, norm2_gain).astype(jnp.bfloat16)
    hidden = jax.nn.gelu(
        jnp.dot(normed2, up_weight, preferred_element_type=jnp.float32), approximate=False
    ).astype(jnp.bfloat16)
    after_mlp = after_attention + lax.psum(
        jnp.dot(hidden, down_weight, preferred_element_type=jnp.float32).astype(jnp.bfloat16), "tp"
    ).astype(jnp.float32)
    final_norm = layer_norm(after_mlp, merge_gain).astype(jnp.bfloat16)
    grouped = final_norm.reshape(group_rows, 4 * final_norm.shape[1])
    merged = jnp.dot(grouped, merge_weight, preferred_element_type=jnp.float32).astype(jnp.bfloat16)
    return pick_rows(
        merged_targets, jnp.zeros_like(merged), lax.all_gather(merged, "blk", axis=0, tiled=True)
    )


def solution(mesh):
    return jax.shard_map(
        body,
        mesh=mesh,
        in_specs=(
            P("blk", "tp"),
            P(),
            P(),
            P(),
            P(),
            P(None, None, "tp"),
            P("tp", None),
            P(),
            P(None, "tp"),
            P("tp", None),
            P(),
            P(None, "tp"),
        ),
        out_specs=P("blk", "tp"),
        check_vma=False,
    )
```

profile of v0, /device:TPU:0, one launch (start us, length us, event | category | flops | bytes accessed | tf_op | source)
XLA Modules:
  0.0 403.5 jit_solution(19957439187878041)
XLA Ops:
  6.5 0.7 all-gather.6.cloned.1.call-update
  7.3 24.7 %all-gather.6.cloned.1.call-done = bf16[512,1664]{0,1:T(8,128)(2,1)} async-done(((bf16[512,416]{0,1:T(8,128)(2,1)}), bf16[512,1664]{0,1:T(8,128)(2,1)}) %all-gather.6.cloned.1.call-update) | async-done | bytes 1703952 | tf_op jit(solution)/shard_map/all_gather | solution.py:132
  32.0 2.7 copy.36
  34.8 0.3 convert_reduce_fusion
  35.1 0.6 fusion.28
  35.7 4.9 %fusion.79 = bf16[3,512,416]{1,2,0:T(8,128)(2,1)S(1)} fusion(bf16[1664,3,416]{0,2,1:T(8,128)(2,1)} %param.21, bf16[512,1664]{1,0:T(8,128)(2,1)S(1)} %copy.36, f32[1664]{0:T(1024)S(1)} %copy-done.14, f32[512]{0:T(512)S(1)} %add_rsqrt_fusion.2, f32[512]{0:T(512)S(1)} %broadcast_multiply_fusion.2), kind=kOutput, calls=%fused_computation.96 | convolution fusion | flops 2131410944 | bytes 7145984 | tf_op jit(solution)/shard_map/td,dcf->ctf/dot_general | solution.py:134
  40.6 1.0 fusion.137
  41.7 0.7 all-gather.10.cloned.1.call-update
  42.4 0.5 all-reduce.3.cloned.1.call-start
  43.1 0.1 reduce
  43.2 0.1 select_reduce_fusion
  43.4 0.1 convert_reduce_fusion.1
  43.6 0.7 select_reduce_fusion.1
  44.4 63.5 %all-gather.8.cloned.1.call-done = bf16[1,4096,416]{1,2,0:T(8,128)(2,1)} async-done(((bf16[1,512,416]{1,2,0:T(8,128)(2,1)}), bf16[1,4096,416]{1,2,0:T(8,128)(2,1)}) %all-gather.8.cloned.1.call-update) | async-done | bytes 3407888 | tf_op jit(solution)/shard_map/all_gather | solution.py:145
  107.9 8.2 %reshape.328 = bf16[4,1024,416]{1,0,2:T(4,128)(2,1)} reshape(bf16[1,4096,416]{1,2,0:T(8,128)(2,1)} %all-gather.8.cloned.1.call-done) | data formatting | bytes 6815744 | tf_op jit(solution)/shard_map/reshape | solution.py:153
  116.1 4.9 %copy.37 = bf16[4,1024,416]{1,2,0:T(8,128)(2,1)} copy(bf16[4,1024,416]{1,0,2:T(4,128)(2,1)} %reshape.328) | data formatting | bytes 6815744 | tf_op jit(solution)/shard_map/while | solution.py:169
  121.0 53.2 %all-gather.10.cloned.1.call-done = bf16[1,4096,416]{1,2,0:T(8,128)(2,1)} async-done(((bf16[1,512,416]{1,2,0:T(8,128)(2,1)}), bf16[1,4096,416]{1,2,0:T(8,128)(2,1)}) %all-gather.10.cloned.1.call-update) | async-done | bytes 3407888 | tf_op jit(solution)/shard_map/all_gather | solution.py:146
  174.2 8.2 %reshape.329 = bf16[4,1024,416]{1,0,2:T(4,128)(2,1)} reshape(bf16[1,4096,416]{1,2,0:T(8,128)(2,1)} %all-gather.10.cloned.1.call-done) | data formatting | bytes 6815744 | tf_op jit(solution)/shard_map/reshape | solution.py:154
  182.4 4.8 %copy.38 = bf16[4,1024,416]{1,2,0:T(8,128)(2,1)} copy(bf16[4,1024,416]{1,0,2:T(4,128)(2,1)} %reshape.329) | data formatting | bytes 6815744 | tf_op jit(solution)/shard_map/while | solution.py:169
  187.3 1.0 broadcast_in_dim.167
  188.3 34.9 %while.14 = (s32[]{:T(128)}, f32[4,512]{1,0:T(4,128)S(1)}, f32[4,512]{1,0:T(4,128)S(1)}, f32[512,4,104]{0,2,1:T(8,128)}, s32[512]{0:T(512)S(1)}, /*index=5*/s32[...) while((s32[]{:T(128)}, f32[4,512]{1,0:T(4,128)S(1)}, ...), condition=%wide.region_16.17_spmd, body=%wide.region_10.16_spmd.sunk | while | flops 901683200 | bytes 41472296 | solution.py:169
  188.3 1.0 compare_reduce_fusion.2
  190.0 9.4 %conditional.2 = ((f32[4,512]{1,0:T(4,128)S(1)}, f32[4,512]{1,0:T(4,128)S(1)}, f32[512,4,104]{0,2,1:T(8,128)})) conditional(s32[]{:T(128)} %convert_element_type.172, (f32[4,512]{1,0:T(4,128)S(1)}, f32[4,512]{1,0:T(4,128)S(1)}, f32[512,4,104]{0,2,1:T(8,128)}) %tuple.42, (s32[512]{0:T(512)S(1)}, s32[1024]{0:T(1024)S(1)}, ...), branch_computations={%region_12.12_spmd, %region_13.15_spmd} | conditional | flops 900634624 | bytes 41457756 | solution.py:161
  190.0 0.4 broadcast_compare_fusion
  190.3 1.6 constant_dynamic-slice_fusion
  191.9 1.8 fusion
  193.8 2.1 fusion.2
  195.9 2.5 fusion.9
  198.5 0.9 copy-done.5
  199.4 1.0 compare_reduce_fusion.2
  201.0 9.4 %conditional.2 = ((f32[4,512]{1,0:T(4,128)S(1)}, f32[4,512]{1,0:T(4,128)S(1)}, f32[512,4,104]{0,2,1:T(8,128)})) conditional(s32[]{:T(128)} %convert_element_type.172, (f32[4,512]{1,0:T(4,128)S(1)}, f32[4,512]{1,0:T(4,128)S(1)}, f32[512,4,104]{0,2,1:T(8,128)}) %tuple.42, (s32[512]{0:T(512)S(1)}, s32[1024]{0:T(1024)S(1)}, ...), branch_computations={%region_12.12_spmd, %region_13.15_spmd} | conditional | flops 900634624 | bytes 41457756 | solution.py:161
  201.1 0.4 broadcast_compare_fusion
  201.4 1.6 constant_dynamic-slice_fusion
  203.0 1.8 fusion
  204.8 2.1 fusion.2
  207.0 2.5 fusion.9
  209.5 0.9 copy-done.5
  210.4 1.0 compare_reduce_fusion.2
  212.1 9.4 %conditional.2 = ((f32[4,512]{1,0:T(4,128)S(1)}, f32[4,512]{1,0:T(4,128)S(1)}, f32[512,4,104]{0,2,1:T(8,128)})) conditional(s32[]{:T(128)} %convert_element_type.172, (f32[4,512]{1,0:T(4,128)S(1)}, f32[4,512]{1,0:T(4,128)S(1)}, f32[512,4,104]{0,2,1:T(8,128)}) %tuple.42, (s32[512]{0:T(512)S(1)}, s32[1024]{0:T(1024)S(1)}, ...), branch_computations={%region_12.12_spmd, %region_13.15_spmd} | conditional | flops 900634624 | bytes 41457756 | solution.py:161
  212.1 0.4 broadcast_compare_fusion
  212.5 1.6 constant_dynamic-slice_fusion
  214.1 1.8 fusion
  215.9 2.1 fusion.2
  218.1 2.5 fusion.9
  220.6 0.9 copy-done.5
  221.5 1.0 compare_reduce_fusion.2
  223.2 1.3 divide_convert_fusion
  224.5 2.3 convolution_convert_fusion
  226.9 0.2 all-reduce.5.cloned.1.call-start
  227.1 0.2 select_reduce_fusion.3
  227.5 52.1 %all-reduce.3.cloned.1.call-done = bf16[512,1664]{1,0:T(8,128)(2,1)} async-done(((bf16[512,1664]{1,0:T(8,128)(2,1)}), bf16[512,1664]{1,0:T(8,128)(2,1)}) %all-reduce.3.cloned.1.call-update) | async-done | bytes 1703952 | tf_op jit(solution)/shard_map/psum | solution.py:176
  279.5 2.1 fusion.31
  281.7 0.8 multiply_reduce_fusion.1
  282.5 21.8 %convolution_convert_fusion.1 = bf16[512,1664]{1,0:T(8,128)(2,1)} fusion(bf16[2048,1664]{1,0:T(8,128)(2,1)} %param.25, bf16[1664,2048]{1,0:T(8,128)(2,1)} %param.24, bf16[512,1664]{1,0:T(8,128)(2,1)} %all-reduce.3.cloned.1.call-done, bf16[512,1664]{1,0:T(8,128)(2,1)S(1)} %copy.36, f32[1664]{0:T(1024)S(1)} %copy-done.15, f32[512]{0:T(512)S(1)} %add_rsqrt_fusion.1, ...), kind=kOutput, calls=%fused_computation.54 | convolution fusion | flops 7054295040 | bytes 18754048 | tf_op jit(solution)/shard_map/dot_general | solution.py:184
  304.4 45.0 %all-reduce.5.cloned.1.call-done = bf16[512,1664]{1,0:T(8,128)(2,1)} async-done(((bf16[512,1664]{1,0:T(8,128)(2,1)}), bf16[512,1664]{1,0:T(8,128)(2,1)}) %all-reduce.5.cloned.1.call-update) | async-done | bytes 1703952 | tf_op jit(solution)/shard_map/psum | solution.py:183
  349.5 2.9 fusion.82
  352.5 1.0 multiply_reduce_fusion
  353.4 2.1 multiply_convert_fusion
  355.6 3.0 reshape.330
  358.6 4.2 %convolution_convert_fusion.2 = bf16[128,416]{0,1:T(8,128)(2,1)S(1)} fusion(bf16[128,6656]{1,0:T(8,128)(2,1)S(1)} %reshape.330, bf16[6656,416]{0,1:T(8,128)(2,1)} %param.27), kind=kOutput, calls=%fused_computation.97 | convolution fusion | flops 708890624 | bytes 7348224 | tf_op jit(solution)/shard_map/dot_general | solution.py:188
  362.7 30.9 %all_gather.15 = bf16[1024,416]{0,1:T(8,128)(2,1)} all-gather(bf16[128,416]{0,1:T(8,128)(2,1)S(1)} %convolution_convert_fusion.2), channel_id=1, replica_groups=mesh['blk'=8,'tp'=4] {'blk'}, dimensions={0}, use_global_device_ids=true | all-gather | bytes 958464 | tf_op jit(solution)/shard_map/all_gather | solution.py:190
  393.6 1.4 copy.39
  395.0 0.8 gather_fusion
  396.0 0.8 copy.40
  (83 shorter events, 1.2 us)
Async XLA Ops:
  6.5 218.0 %copy-start = (bf16[416,1664]{1,0:T(8,128)(2,1)S(1)}, bf16[416,1664]{1,0:T(8,128)(2,1)}, u32[]{:S(2)}) copy-start(bf16[416,1664]{1,0:T(8,128)(2,1)} %param.22) | copy-start | bytes 4153348
  6.5 29.2 %copy-start.14 = (f32[1664]{0:T(1024)S(1)}, f32[1664]{0:T(1024)}, u32[]{:S(2)}) copy-start(f32[1664]{0:T(1024)} %param.20) | copy-start | bytes 19972
  6.5 25.5 %all-gather.6.cloned.1.call-start = ((), (), s32[]{:S(2)}) async-start(), calls=%async_computation | async-start | bytes 2129920 | tf_op jit(solution)/shard_map/all_gather | solution.py:132
  7.3 100.6 %all-gather.8.cloned.1.call-start = ((), (), s32[]{:S(2)}) async-start(), calls=%async_computation.3 | async-start | bytes 3833856 | tf_op jit(solution)/shard_map/all_gather | solution.py:145
  35.7 7.2 %copy-start.9 = (s32[32]{0:T(128)S(1)}, s32[32]{0:T(128)}, u32[]{:S(2)}) copy-start(s32[32]{0:T(128)} %param.18) | copy-start | bytes 388
  35.7 7.5 %copy-start.11 = (s32[16]{0:T(128)S(1)}, s32[16]{0:T(128)}, u32[]{:S(2)}) copy-start(s32[16]{0:T(128)} %param.17) | copy-start | bytes 196
  41.7 132.5 %all-gather.10.cloned.1.call-start = ((), (), s32[]{:S(2)}) async-start(), calls=%async_computation.4 | async-start | bytes 3833856 | tf_op jit(solution)/shard_map/all_gather | solution.py:146
  42.4 237.1 %all-reduce.3.cloned.1.call-start = ((), (), s32[]{:S(2)}) async-start(), calls=%async_computation.1 | async-start | bytes 3407872 | tf_op jit(solution)/shard_map/psum | solution.py:176
  43.2 77.8 %copy-start.7 = (s32[32]{0:T(128)}, s32[32]{0:T(128)S(1)}, u32[]{:S(2)}) copy-start(s32[32]{0:T(128)S(1)} %reduce) | copy-start | bytes 388
  193.8 2.1 copy-start.4
  198.4 0.9 copy-start.5
  204.8 2.1 copy-start.4
  209.5 0.9 copy-start.5
  215.9 2.1 copy-start.4
  220.6 0.9 copy-start.5
  224.5 2.6 copy-start.10
  224.5 2.6 copy-start.13
  224.5 2.8 copy-start.8
  226.9 55.6 %copy-start.15 = (f32[1664]{0:T(1024)S(1)}, f32[1664]{0:T(1024)}, u32[]{:S(2)}) copy-start(f32[1664]{0:T(1024)} %param.23) | copy-start | bytes 19972
  226.9 122.6 %all-reduce.5.cloned.1.call-start = ((), (), s32[]{:S(2)}) async-start(), calls=%async_computation.2 | async-start | bytes 3407872 | tf_op jit(solution)/shard_map/psum | solution.py:183
  279.5 2.1 copy-start.1
  282.4 21.8 %copy-start.12 = (s32[16]{0:T(128)S(1)}, s32[16]{0:T(128)}, u32[]{:S(2)}) copy-start(s32[16]{0:T(128)} %param.17) | copy-start | bytes 196
  304.4 49.0 %copy-start.6 = (f32[1664]{0:T(1024)S(1)}, f32[1664]{0:T(1024)}, u32[]{:S(2)}) copy-start(f32[1664]{0:T(1024)} %param.26) | copy-start | bytes 19972
  349.5 2.9 copy-start.2
  349.5 3.0 copy-start.3
Sparse Core Ops, SparseCore 0:
  8.9 23.0 all-gather.5
  41.8 66.0 all-gather.7
  109.9 64.2 all-gather.9
  227.0 52.4 all-reduce.2
  304.4 45.0 all-reduce.4
where the time goes:
time: 408 us; the launch traced here: 404 us
  waiting for transfers between devices  240 us (59%)
  matrix products  46.3 us (11%)
  local copies, waits for them, and re-layouts  44.6 us (11%)
  blocking collectives  30.9 us (8%)
  other arithmetic  24.5 us (6%)
  between operations  13.7 us (3%)
    all_gather x1, waiting for transfers between devices, body(): key_piece = lax.all_gather(projected[1], 'blk', axis=0, tiled=True)  63.5 us
    all_gather x1, waiting for transfers between devices, body(): value_piece = lax.all_gather(projected[2], 'blk', axis=0, tiled=True)  53.2 us
    psum x1, waiting for transfers between devices, body(): lax.psum(jnp.dot(attended, out_weight, preferred_element_type=jnp.float32...  52.1 us
    psum x1, waiting for transfers between devices, body(): lax.psum(jnp.dot(hidden, down_weight, preferred_element_type=jnp.float32)...  45 us
    all_gather x1, blocking collectives, body(): lax.all_gather(merged, 'blk', axis=0, tiled=True)  30.9 us
    all_gather x1, waiting for transfers between devices, body(): features = lax.all_gather(tokens, 'tp', axis=1, tiled=True)  24.7 us
    dot_general x1, matrix products, body(): jnp.dot(hidden, down_weight, preferred_element_type=jnp.float32)  21.8 us
    while x2, local copies, waits for them, and re-layouts, body(): carried, unused = lax.scan(visit_block, carried, stacked)  9.72 us
  transfers between devices with their start and end apart: 5, of which 5 were waited for; matrix products, arithmetic and copies ran while one was open for 4% of the time, Pallas kernels for 0%

commit v1 on v0

v1 whole, which is shorter than its diff:
```python
import jax
import jax.numpy as jnp
from jax import lax
from jax.experimental import pallas as pl
from jax.experimental.pallas import tpu as pltpu
from jax.sharding import PartitionSpec as P

HDIM = 104
EPSILON = 1e-06
MASKED = -1e30
PIECES = 4
TP = 4
MESH = pl.DeviceIdType.MESH


def norm_rows(values, norm_gain):
    row_mean = jnp.mean(values, axis=-1, keepdims=True)
    centred = values - row_mean
    spread = jnp.mean(centred * centred, axis=-1, keepdims=True)
    return centred * lax.rsqrt(spread + EPSILON) * norm_gain


def partners():
    me = lax.axis_index("tp")
    core = lax.rem(me, 2)
    side = me // 2
    near = side * 2 + (1 - core)
    far = (1 - side) * 2 + core
    across = (1 - side) * 2 + (1 - core)
    return me, near, far, across


def greet(near, far):
    barrier = pltpu.get_barrier_semaphore()
    for other in (near, far):
        pl.semaphore_signal(barrier, inc=1, device_id={"tp": other}, device_id_type=MESH)
    pl.semaphore_wait(barrier, 2)


def send(source, target, sems, index, other):
    return pltpu.make_async_remote_copy(
        src_ref=source,
        dst_ref=target,
        send_sem=sems.at[0, index],
        recv_sem=sems.at[1, index],
        device_id={"tp": other},
        device_id_type=MESH,
    )


def gather_kernel(x_ref, gain_ref, out_ref, rest_ref, held, far_sems, near_sems, pass_sems, own_sem):
    me, near, far, across = partners()
    rows = x_ref.shape[0]
    own_rows = rest_ref.shape[0]
    size = rows // PIECES
    own_copy = pltpu.make_async_copy(x_ref, held.at[me], own_sem)
    own_copy.start()
    greet(near, far)
    to_far, to_near, passed = [], [], []
    for i in range(PIECES):
        part = pl.ds(i * size, size)
        to_far.append(send(x_ref.at[part], held.at[me, part], far_sems, i, far))
        to_far[i].start()
    for i in range(PIECES):
        part = pl.ds(i * size, size)
        to_near.append(send(x_ref.at[part], held.at[me, part], near_sems, i, near))
        to_near[i].start()
    for i in range(PIECES):
        part = pl.ds(i * size, size)
        to_far[i].wait_recv()
        passed.append(send(held.at[far, part], held.at[far, part], pass_sems, i, near))
        passed[i].start()
    own_copy.wait()
    for i in range(PIECES):
        to_near[i].wait_recv()
        passed[i].wait_recv()
        for j in range(0, size, 64):
            part = pl.ds(i * size + j, 64)
            values = jnp.concatenate(
                [held[k, part].astype(jnp.float32) for k in range(TP)], axis=1
            )
            out_ref[part] = norm_rows(values, gain_ref[...]).astype(jnp.bfloat16)
    for j in range(0, own_rows, 64):
        part = pl.ds(pl.multiple_of(me * own_rows + j, 64), 64)
        rest_ref[pl.ds(j, 64)] = jnp.concatenate(
            [held[k, part].astype(jnp.float32) for k in range(TP)], axis=1
        )
    for i in range(PIECES):
        to_far[i].wait_send()
        to_near[i].wait_send()
        passed[i].wait_send()


def sum_kernel(
    part_ref, rest_ref, gain_ref, out_ref, after_ref,
    got_far, got_own, forward, got_side, sems,
):
    me, near, far, across = partners()
    own_rows = rest_ref.shape[0]
    size = own_rows // PIECES

    def rows(chunk, i):
        return pl.ds(pl.multiple_of(chunk * own_rows + i * size, size), size)

    greet(near, far)
    first, second, third, fourth, fifth, sixth = [], [], [], [], [], []
    for i in range(PIECES):
        here = pl.ds(i * size, size)
        first.append(send(part_ref.at[rows(across, i)], got_far.at[here], sems.at[0], i, near))
        first[i].start()
    for i in range(PIECES):
        here = pl.ds(i * size, size)
        second.append(send(part_ref.at[rows(near, i)], got_own.at[here], sems.at[1], i, near))
        second[i].start()
    for i in range(PIECES):
        here = pl.ds(i * size, size)
        first[i].wait_recv()
        forward[here] = (
            part_ref[rows(far, i)].astype(jnp.float32) + got_far[here].astype(jnp.float32)
        ).astype(jnp.bfloat16)
        third.append(send(forward.at[here], got_side.at[here], sems.at[2], i, far))
        third[i].start()
    for i in range(PIECES):
        here = pl.ds(i * size, size)
        second[i].wait_recv()
        third[i].wait_recv()
        total = rest_ref[here] + (
            part_ref[rows(me, i)].astype(jnp.float32)
            + got_own[here].astype(jnp.float32)
            + got_side[here].astype(jnp.float32)
        )
        after_ref[here] = total
        out_ref[rows(me, i)] = norm_rows(total, gain_ref[...]).astype(jnp.bfloat16)
        fourth.append(send(out_ref.at[rows(me, i)], out_ref.at[rows(me, i)], sems.at[3], i, far))
        fourth[i].start()
        fifth.append(send(out_ref.at[rows(me, i)], out_ref.at[rows(me, i)], sems.at[4], i, near))
        fifth[i].start()
    for i in range(PIECES):
        fourth[i].wait_recv()
        sixth.append(send(out_ref.at[rows(far, i)], out_ref.at[rows(far, i)], sems.at[5], i, near))
        sixth[i].start()
    for i in range(PIECES):
        fifth[i].wait_recv()
        sixth[i].wait_recv()
    for i in range(PIECES):
        for copies in (first, second, third, fourth, fifth, sixth):
            copies[i].wait_send()


def vmem(count):
    return [pl.BlockSpec(memory_space=pltpu.VMEM)] * count


def gather_norm(x, gain, collective_id):
    rows, width = x.shape
    full = width * TP
    pair = pltpu.SemaphoreType.DMA((2, PIECES))
    return pl.pallas_call(
        gather_kernel,
        out_shape=(
            jax.ShapeDtypeStruct((rows, full), jnp.bfloat16),
            jax.ShapeDtypeStruct((rows // TP, full), jnp.float32),
        ),
        in_specs=vmem(2),
        out_specs=tuple(vmem(2)),
        scratch_shapes=[
            pltpu.VMEM((TP, rows, width), jnp.bfloat16),
            pair, pair, pair, pltpu.SemaphoreType.DMA,
        ],
        compiler_params=pltpu.CompilerParams(
            collective_id=collective_id, has_side_effects=True, vmem_limit_bytes=40 * 2**20
        ),
        name="gather_norm",
    )(x, gain.reshape(1, -1))


def sum_norm(part, rest, gain, collective_id):
    rows, full = part.shape
    own = (rows // TP, full)
    return pl.pallas_call(
        sum_kernel,
        out_shape=(
            jax.ShapeDtypeStruct((rows, full), jnp.bfloat16),
            jax.ShapeDtypeStruct(own, jnp.float32),
        ),
        in_specs=vmem(3),
        out_specs=tuple(vmem(2)),
        scratch_shapes=[pltpu.VMEM(own, jnp.bfloat16)] * 4
        + [pltpu.SemaphoreType.DMA((6, 2, PIECES))],
        compiler_params=pltpu.CompilerParams(
            collective_id=collective_id, has_side_effects=True, vmem_limit_bytes=40 * 2**20
        ),
        name="sum_norm",
    )(part, rest, gain.reshape(1, -1))


def route(tokens, block_split, req_lengths, req_owners):
    count = lax.axis_size("blk")
    rows, width = tokens.shape
    groups = rows // 4
    block_groups = groups // 2
    each = groups // count
    requests = req_lengths.shape[0]
    room = (groups + (requests // count) * (count - 1)) // count
    room = (room + 3) // 4 * 4
    index = lax.axis_index("blk")
    position = jnp.arange(requests, dtype=jnp.int32)
    ends = jnp.sum(
        jnp.where(position[None, :] <= position[:, None], req_lengths[None, :], 0), axis=1
    )
    starts = ends - req_lengths
    earlier = (req_owners[None, :] == req_owners[:, None]) & (position[None, :] < position[:, None])
    offset = jnp.sum(jnp.where(earlier, req_lengths[None, :], 0), axis=1)
    spot = jnp.arange(groups, dtype=jnp.int32)
    local = (spot % each) * count + index
    place = (spot // each) * 2 + local // block_groups
    places = jnp.arange(block_split.shape[0], dtype=jnp.int32)
    block = jnp.sum(jnp.where(place[:, None] == places[None, :], block_split[None, :], 0), axis=1)
    packed = block * block_groups + local % block_groups
    inside = (starts[None, :] <= packed[:, None]) & (packed[:, None] < ends[None, :])
    goal = jnp.sum(
        jnp.where(inside, (req_owners * groups + offset - starts)[None, :], 0), axis=1
    ) + packed
    owner = goal // groups
    rank = jnp.sum(
        ((owner[None, :] == owner[:, None]) & (goal[None, :] < goal[:, None])).astype(jnp.int32),
        axis=1,
    )
    out_spot = owner * room + rank
    chosen = (
        (req_owners[None, :] == index)
        & (offset[None, :] <= spot[:, None])
        & (spot[:, None] < (offset + req_lengths)[None, :])
    )
    wanted = jnp.sum(jnp.where(chosen, (starts - offset)[None, :], 0), axis=1) + spot
    request = jnp.sum(jnp.where(chosen, position[None, :], 0), axis=1)
    via = wanted % count
    turn = jnp.sum(
        ((via[None, :] == via[:, None]) & (spot[None, :] < spot[:, None])).astype(jnp.int32), axis=1
    )
    in_spot = via * room + turn

    def pick(hot, array):
        return jnp.dot(
            hot.astype(jnp.bfloat16), array, preferred_element_type=jnp.float32
        ).astype(jnp.bfloat16)

    row = jnp.arange(rows, dtype=jnp.int32)
    via_row = row // (4 * each)
    q_row = row // 4 % each
    source = (q_row * count + via_row) * 4 + row % 4
    sent = pick(source[:, None] == row[None, :], tokens)
    held = lax.all_to_all(sent, "blk", 0, 0, tiled=True)
    row_goal = jnp.repeat(out_spot, 4) * 4 + row % 4
    slots = jnp.arange(count * room * 4, dtype=jnp.int32)
    sent = pick(slots[:, None] == row_goal[None, :], held)
    held = lax.all_to_all(sent, "blk", 0, 0, tiled=True)
    row_from = jnp.tile(in_spot, 4) * 4 + row // groups
    return pick(row_from[:, None] == slots[None, :], held), request


def body(
    tokens,
    block_split,
    req_lengths,
    req_owners,
    norm1_gain,
    qkv_weight,
    out_weight,
    norm2_gain,
    up_weight,
    down_weight,
    merge_gain,
    merge_weight,
):
    rows, width = tokens.shape
    groups = rows // 4
    routed, request = route(tokens, block_split, req_lengths, req_owners)
    normed1, rest = gather_norm(routed, norm1_gain, 1)
    projected = jnp.einsum(
        "td,dcf->ctf", normed1, qkv_weight, preferred_element_type=jnp.float32
    ).astype(jnp.bfloat16)
    heads = width // HDIM
    queries, keys, values = (projected[c].reshape(rows, heads, HDIM) for c in range(3))
    segment = jnp.tile(request, 4)
    same = (segment[:, None] == segment[None, :])[None, :, :]
    scores = jnp.einsum(
        "qhd,khd->hqk", queries, keys, preferred_element_type=jnp.float32
    ) * HDIM ** (-0.5)
    scores = jnp.where(same, scores, MASKED)
    weights = jnp.exp(scores - jnp.max(scores, axis=2, keepdims=True))
    totals = jnp.sum(weights, axis=2)
    mixed = jnp.einsum(
        "hqk,khd->qhd", weights.astype(jnp.bfloat16), values, preferred_element_type=jnp.float32
    )
    attended = (mixed / jnp.transpose(totals)[:, :, None]).reshape(rows, width).astype(jnp.bfloat16)
    part = jnp.dot(attended, out_weight, preferred_element_type=jnp.float32).astype(jnp.bfloat16)
    normed2, rest = sum_norm(part, rest, norm2_gain, 2)
    hidden = jax.nn.gelu(
        jnp.dot(normed2, up_weight, preferred_element_type=jnp.float32), approximate=False
    ).astype(jnp.bfloat16)
    part = jnp.dot(hidden, down_weight, preferred_element_type=jnp.float32).astype(jnp.bfloat16)
    final, unused = sum_norm(part, rest, merge_gain, 3)
    full = final.shape[1]
    merged = jnp.zeros((groups, merge_weight.shape[1]), jnp.float32)
    for k in range(4):
        merged = merged + jnp.dot(
            final[k * groups : (k + 1) * groups],
            merge_weight[k * full : (k + 1) * full],
            preferred_element_type=jnp.float32,
        )
    return merged.astype(jnp.bfloat16)


def solution(mesh):
    return jax.shard_map(
        body,
        mesh=mesh,
        in_specs=(
            P("blk", "tp"),
            P(),
            P(),
            P(),
            P(),
            P(None, None, "tp"),
            P("tp", None),
            P(),
            P(None, "tp"),
            P("tp", None),
            P(),
            P(None, "tp"),
        ),
        out_specs=P("blk", "tp"),
        check_vma=False,
    )
```

time: 408 us -> 154 us (0.38); the launches traced: 404 us -> 154 us
  waiting for transfers between devices: 240 us -> 27.2 us
  Pallas kernels: 0 us -> 65 us
  local copies, waits for them, and re-layouts: 44.6 us -> 5.83 us
  blocking collectives: 30.9 us -> 0 us
  other arithmetic: 24.5 us -> 5.33 us
  between operations: 13.7 us -> 0.25 us
  starting transfers between devices: 0.8 us -> 10.9 us
  matrix products: 46.3 us -> 39.2 us
    all_gather x3 -> x0, waiting for transfers between devices: 141 us -> none  [the longest x1 63.5 us: body(): key_piece = lax.all_gather(projected[1], 'blk', axis=0, tiled=True)]
    psum x2 -> x0, waiting for transfers between devices: 97.1 us -> none  [the longest x1 52.1 us: body(): lax.psum(jnp.dot(attended, out_weight, preferred_element_type=jnp.float32...]
    pallas_call x0 -> x3, Pallas kernels: none -> 65 us  [the longest x2 48.5 us: sum_norm(): pl.pallas_call(sum_kernel, out_shape=(jax.ShapeDtypeStruct((rows, full),...]
    all_gather x1 -> x0, blocking collectives: 30.9 us -> none  [body(): lax.all_gather(merged, 'blk', axis=0, tiled=True)]
    all_to_all x0 -> x2, waiting for transfers between devices: none -> 27.2 us  [route(): held = lax.all_to_all(sent, 'blk', 0, 0, tiled=True)]
    reshape x4 -> x3, local copies, waits for them, and re-layouts: 19.4 us -> 0.02 us  [the longest x2 0.01 us: sum_norm(): gain.reshape(1, -1)]
    reduce_sum x16 -> x6, other arithmetic: 15.4 us -> 3.03 us  [the longest x1 0.92 us: body(): totals = jnp.sum(weights, axis=2)]
    all_to_all x0 -> x2, starting transfers between devices: none -> 10.9 us  [route(): held = lax.all_to_all(sent, 'blk', 0, 0, tiled=True)]
  transfers between devices with their start and end apart: 5 -> 2, of which waited for: 5 -> 2; matrix products, arithmetic and copies ran while one was open for 4% -> 3% of each run, Pallas kernels for 0% -> 0%
where the time goes in v1:
time: 154 us
  Pallas kernels  65 us (42%)
  matrix products  39.2 us (25%)
  waiting for transfers between devices  27.2 us (18%)
  starting transfers between devices  10.9 us (7%)
  local copies, waits for them, and re-layouts  5.83 us (4%)
  other arithmetic  5.33 us (3%)
    pallas_call x2, Pallas kernels, sum_norm(): pl.pallas_call(sum_kernel, out_shape=(jax.ShapeDtypeStruct((rows, full),...  48.5 us
    all_to_all x2, waiting for transfers between devices, route(): held = lax.all_to_all(sent, 'blk', 0, 0, tiled=True)  27.2 us
    dot_general x1, matrix products, body(): jnp.dot(hidden, down_weight, preferred_element_type=jnp.float32)  20 us
    pallas_call x1, Pallas kernels, gather_norm(): pl.pallas_call(gather_kernel, out_shape=(jax.ShapeDtypeStruct((rows, full...  16.5 us
    all_to_all x2, starting transfers between devices, route(): held = lax.all_to_all(sent, 'blk', 0, 0, tiled=True)  10.9 us
    dot_general x4, matrix products, body(): jnp.dot(final[k * groups:(k + 1) * groups], merge_weight[k * full:(k + 1)...  8.12 us
    dot_general x1, matrix products, body(): jnp.einsum('td,dcf->ctf', normed1, qkv_weight, preferred_element_type=jnp...  4.69 us
    unnamed x14, local copies, waits for them, and re-layouts  3.24 us
  transfers between devices with their start and end apart: 2, of which 2 were waited for; matrix products, arithmetic and copies ran while one was open for 3% of the time, Pallas kernels for 0%

profile of v1, /device:TPU:0, one launch (start us, length us, event | category | flops | bytes accessed | tf_op | source)
XLA Modules:
  0.0 153.7 jit_solution(13342432786075904670)
XLA Ops:
  0.0 0.0 copy-start
  0.0 0.0 copy-start.4
  0.0 0.0 copy-start.5
  0.0 0.0 copy-start.6
  0.0 1.7 %convolution_convert_fusion.2 = bf16[512,416]{0,1:T(8,128)(2,1)S(1)} fusion(bf16[512,416]{0,1:T(8,128)(2,1)} %param.12, s32[512]{0:T(512)S(1)} %fusion.104), kind=kOutput, calls=%fused_computation.77 | convolution fusion | flops 218578944 | bytes 854016 | tf_op jit(solution)/shard_map/dot_general | solution.py:244
  1.7 1.0 copy.23
  2.7 7.3 %all-to-all-start = ((bf16[8,64,416]{2,1,0:T(8,128)(2,1)}), bf16[8,64,416]{2,1,0:T(8,128)(2,1)S(1)}, u32[]{:S(2)}, u32[]{:S(2)}) async-start(bf16[8,64,416]{2,1,0:T(8,128)(2,1)} %bitcast.1), calls=%async_computation | async-start | bytes 1048576 | tf_op jit(solution)/shard_map/all_to_all | solution.py:253
  10.0 0.7 broadcast_compare_fusion.1
  10.7 0.9 select_reduce_fusion.4
  11.6 0.7 fusion.152
  12.2 0.7 add_subtract_fusion
  12.9 0.7 select_reduce_fusion.5
  13.6 0.1 select_reduce_fusion
  13.8 0.2 convert_reduce_fusion
  14.0 0.1 broadcast_in_dim.114
  14.0 0.1 mul.142
  14.2 10.3 %all-to-all-done = bf16[8,64,416]{2,1,0:T(8,128)(2,1)S(1)} async-done(((bf16[8,64,416]{2,1,0:T(8,128)(2,1)}), bf16[8,64,416]{2,1,0:T(8,128)(2,1)S(1)}, u32[]{:S(2)}, u32[]{:S(2)}) %all-to-all-start) | async-done | bytes 426016 | tf_op jit(solution)/shard_map/all_to_all | solution.py:253
  24.5 0.6 fusion.68
  25.0 1.1 copy.24
  26.1 3.6 %all-to-all-start.1 = ((bf16[8,80,416]{2,1,0:T(8,128)(2,1)}), bf16[8,80,416]{2,1,0:T(8,128)(2,1)S(1)}, u32[]{:S(2)}, u32[]{:S(2)}) async-start(bf16[8,80,416]{2,1,0:T(8,128)(2,1)} %bitcast.3), calls=%async_computation.1 | async-start | bytes 1310720 | tf_op jit(solution)/shard_map/all_to_all | solution.py:257
  29.8 0.2 convert_reduce_fusion.1
  29.9 0.0 copy-done.4
  30.0 0.0 copy-done.5
  30.0 0.0 copy-done.6
  30.0 0.2 broadcast_compare_fusion
  30.3 17.0 %all-to-all-done.1 = bf16[8,80,416]{2,1,0:T(8,128)(2,1)S(1)} async-done(((bf16[8,80,416]{2,1,0:T(8,128)(2,1)}), bf16[8,80,416]{2,1,0:T(8,128)(2,1)S(1)}, u32[]{:S(2)}, u32[]{:S(2)}) %all-to-all-start.1) | async-done | bytes 532512 | tf_op jit(solution)/shard_map/all_to_all | solution.py:257
  47.2 0.7 fusion.69
  47.9 0.2 copy.25.x_ref
  48.1 16.5 %gather_norm.1 = (bf16[512,1664]{1,0:T(8,128)(2,1)S(1)}, f32[128,1664]{1,0:T(8,128)S(1)}) custom-call(bf16[512,416]{1,0:T(8,128)(2,1)S(1)} %copy.25.x_ref, f32[1,1664]{1,0:T(1,128)S(1)} %reshape.319.gain_ref), custom_call_target="tpu_custom_call" | custom-call | tf_op jit(solution)/shard_map/gather_norm/pallas_call | solution.py:158
  64.6 4.7 %fusion.52 = bf16[3,512,416]{1,2,0:T(8,128)(2,1)S(1)} fusion(bf16[1664,3,416]{0,2,1:T(8,128)(2,1)} %param.17, bf16[512,1664]{1,0:T(8,128)(2,1)S(1)} %get-tuple-element.10), kind=kOutput, calls=%fused_computation.61 | convolution fusion | flops 2127151104 | bytes 7135232 | tf_op jit(solution)/shard_map/td,dcf->ctf/dot_general | solution.py:280
  69.3 0.1 fusion.153
  69.4 1.0 fusion.10
  70.4 0.9 fusion.11
  71.3 1.3 fusion.85
  72.7 0.0 copy-done
  72.7 1.1 convolution_convert_fusion.part_ref
  73.8 23.7 %sum_norm.2 = (bf16[512,1664]{1,0:T(8,128)(2,1)S(1)}, f32[128,1664]{1,0:T(8,128)S(1)}) custom-call(bf16[512,1664]{1,0:T(8,128)(2,1)S(1)} %convolution_convert_fusion.part_ref, f32[128,1664]{1,0:T(8,128)S(1)} %get-tuple-element.11.rest_ref, f32[1,1664]{1,0:T(1,128)S(1)} %reshape.320.gain_ref), custom_call_target="tpu_custom_call" | custom-call | tf_op jit(solution)/shard_map/sum_norm/pallas_call | solution.py:180
  97.5 0.0 copy-start.1
  97.6 0.9 copy-done.1
  98.4 0.0 copy-start.3
  98.4 1.2 copy-done.3
  99.6 20.0 %convolution_convert_fusion.1.part_ref = bf16[512,1664]{1,0:T(8,128)(2,1)S(1)} fusion(bf16[2048,1664]{1,0:T(8,128)(2,1)} %param.21, bf16[512,1664]{1,0:T(8,128)(2,1)} %copy-done.3, bf16[1664,2048]{1,0:T(8,128)(2,1)} %param.20), kind=kOutput, calls=%fused_computation.25 | convolution fusion | flops 7048331264 | bytes 17039360 | tf_op jit(solution)/shard_map/dot_general | solution.py:302
  119.6 0.0 copy-start.2
  119.6 1.1 copy-done.2
  120.8 24.8 %sum_norm.3 = (bf16[512,1664]{1,0:T(8,128)(2,1)S(1)}, f32[128,1664]{1,0:T(8,128)}) custom-call(bf16[512,1664]{1,0:T(8,128)(2,1)S(1)} %convolution_convert_fusion.1.part_ref, f32[128,1664]{1,0:T(8,128)S(1)} %copy-done.2, f32[1,1664]{1,0:T(1,128)S(1)} %reshape.321.gain_ref), custom_call_target="tpu_custom_call" | custom-call | tf_op jit(solution)/shard_map/sum_norm/pallas_call | solution.py:180
  145.6 1.9 %fusion.59 = f32[128,416]{0,1:T(8,128)S(1)} fusion(bf16[6656,416]{0,1:T(8,128)(2,1)} %param.23, bf16[512,1664]{1,0:T(8,128)(2,1)S(1)} %get-tuple-element.14), kind=kOutput, calls=%fused_computation.66 | convolution fusion | flops 177209344 | bytes 2023424 | tf_op jit(solution)/shard_map/dot_general | solution.py:307
  147.5 1.9 %fusion.70 = f32[128,416]{0,1:T(8,128)S(1)} fusion(f32[128,416]{0,1:T(8,128)S(1)} %fusion.59, bf16[6656,416]{0,1:T(8,128)(2,1)} %param.23, bf16[512,1664]{1,0:T(8,128)(2,1)S(1)} %get-tuple-element.14), kind=kOutput, calls=%fused_computation.78 | convolution fusion | flops 177262592 | bytes 2236416 | tf_op jit(solution)/shard_map/dot_general | solution.py:307
  149.3 1.9 %fusion.73 = f32[128,416]{0,1:T(8,128)S(1)} fusion(f32[128,416]{0,1:T(8,128)S(1)} %fusion.70, bf16[6656,416]{0,1:T(8,128)(2,1)} %param.23, bf16[512,1664]{1,0:T(8,128)(2,1)S(1)} %get-tuple-element.14), kind=kOutput, calls=%fused_computation.79 | convolution fusion | flops 177262592 | bytes 2236416 | tf_op jit(solution)/shard_map/dot_general | solution.py:307
  151.2 2.5 %fusion.79 = bf16[128,416]{0,1:T(8,128)(2,1)} fusion(f32[128,416]{0,1:T(8,128)S(1)} %fusion.73, bf16[6656,416]{0,1:T(8,128)(2,1)} %param.23, bf16[512,1664]{1,0:T(8,128)(2,1)S(1)} %get-tuple-element.14), kind=kOutput, calls=%fused_computation.81 | convolution fusion | flops 177315840 | bytes 2129920 | tf_op jit(solution)/shard_map/dot_general | solution.py:307
  (13 shorter events, 0.1 us)
Async XLA Ops:
  0.0 72.7 %copy-start = (bf16[416,1664]{1,0:T(8,128)(2,1)S(1)}, bf16[416,1664]{1,0:T(8,128)(2,1)}, u32[]{:S(2)}) copy-start(bf16[416,1664]{1,0:T(8,128)(2,1)} %param.18) | copy-start | bytes 4153348
  0.0 29.9 %copy-start.4 = (f32[1664]{0:T(1024)S(1)}, f32[1664]{0:T(1024)}, u32[]{:S(2)}) copy-start(f32[1664]{0:T(1024)} %param.16) | copy-start | bytes 19972
  0.0 30.0 %copy-start.5 = (f32[1664]{0:T(1024)S(1)}, f32[1664]{0:T(1024)}, u32[]{:S(2)}) copy-start(f32[1664]{0:T(1024)} %param.19) | copy-start | bytes 19972
  0.0 30.0 %copy-start.6 = (f32[1664]{0:T(1024)S(1)}, f32[1664]{0:T(1024)}, u32[]{:S(2)}) copy-start(f32[1664]{0:T(1024)} %param.22) | copy-start | bytes 19972
  2.7 21.8 %all-to-all-start = ((bf16[8,64,416]{2,1,0:T(8,128)(2,1)}), bf16[8,64,416]{2,1,0:T(8,128)(2,1)S(1)}, u32[]{:S(2)}, u32[]{:S(2)}) async-start(bf16[8,64,416]{2,1,0:T(8,128)(2,1)} %bitcast.1), calls=%async_computation | async-start | bytes 1048576 | tf_op jit(solution)/shard_map/all_to_all | solution.py:253
  26.1 21.1 %all-to-all-start.1 = ((bf16[8,80,416]{2,1,0:T(8,128)(2,1)}), bf16[8,80,416]{2,1,0:T(8,128)(2,1)S(1)}, u32[]{:S(2)}, u32[]{:S(2)}) async-start(bf16[8,80,416]{2,1,0:T(8,128)(2,1)} %bitcast.3), calls=%async_computation.1 | async-start | bytes 1310720 | tf_op jit(solution)/shard_map/all_to_all | solution.py:257
  97.5 0.9 copy-start.1
  98.4 1.2 copy-start.3
  119.6 1.2 copy-start.2

commit v2 on v1

--- a/solution.py
+++ b/solution.py
@@ -147,6 +147,154 @@
             copies[i].wait_send()
 
 
+def sum_merge_kernel(
+    part_ref, rest_ref, gain_ref, weight_ref, merged_ref,
+    out_ref, weight, got_far, got_own, forward, got_side, sems, weight_sem,
+):
+    me, near, far, across = partners()
+    own_rows = rest_ref.shape[0]
+    size = own_rows // PIECES
+
+    def rows(chunk, i):
+        return pl.ds(pl.multiple_of(chunk * own_rows + i * size, size), size)
+
+    fetch = pltpu.make_async_copy(weight_ref, weight, weight_sem)
+    fetch.start()
+    greet(near, far)
+    first, second, third, fourth, fifth, sixth = [], [], [], [], [], []
+    for i in range(PIECES):
+        here = pl.ds(i * size, size)
+        first.append(send(part_ref.at[rows(across, i)], got_far.at[here], sems.at[0], i, near))
+        first[i].start()
+    for i in range(PIECES):
+        here = pl.ds(i * size, size)
+        second.append(send(part_ref.at[rows(near, i)], got_own.at[here], sems.at[1], i, near))
+        second[i].start()
+    for i in range(PIECES):
+        here = pl.ds(i * size, size)
+        first[i].wait_recv()
+        forward[here] = (
+            part_ref[rows(far, i)].astype(jnp.float32) + got_far[here].astype(jnp.float32)
+        ).astype(jnp.bfloat16)
+        third.append(send(forward.at[here], got_side.at[here], sems.at[2], i, far))
+        third[i].start()
+    for i in range(PIECES):
+        here = pl.ds(i * size, size)
+        second[i].wait_recv()
+        third[i].wait_recv()
+        total = rest_ref[here] + (
+            part_ref[rows(me, i)].astype(jnp.float32)
+            + got_own[here].astype(jnp.float32)
+            + got_side[here].astype(jnp.float32)
+        )
+        out_ref[rows(me, i)] = norm_rows(total, gain_ref[...]).astype(jnp.bfloat16)
+        fourth.append(send(out_ref.at[rows(me, i)], out_ref.at[rows(me, i)], sems.at[3], i, far))
+        fourth[i].start()
+        fifth.append(send(out_ref.at[rows(me, i)], out_ref.at[rows(me, i)], sems.at[4], i, near))
+        fifth[i].start()
+    full = out_ref.shape[1]
+
+    def term(chunk):
+        return lax.dot_general(
+            out_ref[pl.ds(pl.multiple_of(chunk * own_rows, own_rows), own_rows)],
+            weight[:, pl.ds(pl.multiple_of(chunk * full, 128), full)],
+            (((1,), (1,)), ((), ())),
+            preferred_element_type=jnp.float32,
+        )
+
+    fetch.wait()
+    merged = term(me)
+    for i in range(PIECES):
+        fourth[i].wait_recv()
+        sixth.append(send(out_ref.at[rows(far, i)], out_ref.at[rows(far, i)], sems.at[5], i, near))
+        sixth[i].start()
+    merged = merged + term(far)
+    for i in range(PIECES):
+        fifth[i].wait_recv()
+    merged = merged + term(near)
+    for i in range(PIECES):
+        sixth[i].wait_recv()
+    merged_ref[...] = (merged + term(across)).astype(jnp.bfloat16)
+    for i in range(PIECES):
+        for copies in (first, second, third, fourth, fifth, sixth):
+            copies[i].wait_send()
+
+
+def mlp_kernel(x_ref, up_ref, down_ref, out_ref, lifted, total):
+    step = pl.program_id(0)
+    last = pl.num_programs(0) - 1
+
+    def lift():
+        return jnp.dot(x_ref[...], up_ref[...], preferred_element_type=jnp.float32)
+
+    def lower(values):
+        hidden = 0.5 * values * (1.0 + lax.erf(values * (0.5**0.5)))
+        return jnp.dot(
+            hidden.astype(jnp.bfloat16), down_ref[...], preferred_element_type=jnp.float32
+        )
+
+    @pl.when(step == 0)
+    def _():
+        total[...] = jnp.zeros_like(total)
+        lifted[...] = lift()
+
+    @pl.when((step > 0) & (step < last))
+    def _():
+        values = lifted[...]
+        later = lift()
+        total[...] += lower(values)
+        lifted[...] = later
+
+    @pl.when(step == last)
+    def _():
+        out_ref[...] = (total[...] + lower(lifted[...])).astype(jnp.bfloat16)
+
+
+def route_kernel(sent_ref, hot_ref, pick_ref, out_ref, first, second, third, sems):
+    count = lax.axis_size("blk")
+    me = lax.axis_index("blk")
+    others = [lax.rem(me + step, count) for step in range(1, count)]
+    barrier = pltpu.get_barrier_semaphore()
+    for other in others:
+        pl.semaphore_signal(barrier, inc=1, device_id={"blk": other}, device_id_type=MESH)
+    pl.semaphore_wait(barrier, count - 1)
+
+    def hop(source, target, number):
+        size = source.shape[0] // count
+
+        def rows(index):
+            return pl.ds(pl.multiple_of(index * size, size), size)
+
+        copies = []
+        for step, other in enumerate(others):
+            copies.append(
+                pltpu.make_async_remote_copy(
+                    src_ref=source.at[rows(other)],
+                    dst_ref=target.at[rows(me)],
+                    send_sem=sems.at[number, 0, step],
+                    recv_sem=sems.at[number, 1, step],
+                    device_id={"blk": other},
+                    device_id_type=MESH,
+                )
+            )
+            copies[step].start()
+        target[rows(me)] = source[rows(me)]
+        for copy in copies:
+            copy.wait_recv()
+        return copies
+
+    one = hop(sent_ref, first, 0)
+    second[...] = jnp.dot(
+        hot_ref[...], first[...], preferred_element_type=jnp.float32
+    ).astype(jnp.bfloat16)
+    two = hop(second, third, 1)
+    out_ref[...] = jnp.dot(
+        pick_ref[...], third[...], preferred_element_type=jnp.float32
+    ).astype(jnp.bfloat16)
+    for copy in one + two:
+        copy.wait_send()
+
+
 def vmem(count):
     return [pl.BlockSpec(memory_space=pltpu.VMEM)] * count
 
@@ -192,6 +340,71 @@
         ),
         name="sum_norm",
     )(part, rest, gain.reshape(1, -1))
+
+
+def sum_merge(part, rest, gain, weight, collective_id):
+    rows, full = part.shape
+    own = (rows // TP, full)
+    return pl.pallas_call(
+        sum_merge_kernel,
+        out_shape=jax.ShapeDtypeStruct((rows // TP, weight.shape[0]), jnp.bfloat16),
+        in_specs=vmem(3) + [pl.BlockSpec(memory_space=pl.ANY)],
+        out_specs=vmem(1)[0],
+        scratch_shapes=[
+            pltpu.VMEM(part.shape, jnp.bfloat16),
+            pltpu.VMEM(weight.shape, jnp.bfloat16),
+        ]
+        + [pltpu.VMEM(own, jnp.bfloat16)] * 4
+        + [pltpu.SemaphoreType.DMA((6, 2, PIECES)), pltpu.SemaphoreType.DMA],
+        compiler_params=pltpu.CompilerParams(
+            collective_id=collective_id, has_side_effects=True, vmem_limit_bytes=40 * 2**20
+        ),
+        name="sum_merge",
+    )(part, rest, gain.reshape(1, -1), weight)
+
+
+def mlp(x, up, down):
+    rows, full = x.shape
+    tile = 512
+    steps = up.shape[1] // tile
+    return pl.pallas_call(
+        mlp_kernel,
+        grid=(steps + 1,),
+        out_shape=jax.ShapeDtypeStruct((rows, full), jnp.bfloat16),
+        in_specs=[
+            pl.BlockSpec((rows, full), lambda i: (0, 0)),
+            pl.BlockSpec((full, tile), lambda i: (0, jnp.minimum(i, steps - 1))),
+            pl.BlockSpec((tile, full), lambda i: (jnp.maximum(i - 1, 0), 0)),
+        ],
+        out_specs=pl.BlockSpec((rows, full), lambda i: (0, 0)),
+        scratch_shapes=[
+            pltpu.VMEM((rows, tile), jnp.float32),
+            pltpu.VMEM((rows, full), jnp.float32),
+        ],
+        compiler_params=pltpu.CompilerParams(vmem_limit_bytes=40 * 2**20),
+        name="mlp",
+    )(x, up, down)
+
+
+def route_rows(sent, hot, pick, collective_id):
+    count = lax.axis_size("blk")
+    wide = (hot.shape[0], sent.shape[1])
+    return pl.pallas_call(
+        route_kernel,
+        out_shape=jax.ShapeDtypeStruct(sent.shape, jnp.bfloat16),
+        in_specs=vmem(3),
+        out_specs=vmem(1)[0],
+        scratch_shapes=[
+            pltpu.VMEM(sent.shape, jnp.bfloat16),
+            pltpu.VMEM(wide, jnp.bfloat16),
+            pltpu.VMEM(wide, jnp.bfloat16),
+            pltpu.SemaphoreType.DMA((2, 2, count - 1)),
+        ],
+        compiler_params=pltpu.CompilerParams(
+            collective_id=collective_id, has_side_effects=True, vmem_limit_bytes=40 * 2**20
+        ),
+        name="route_rows",
+    )(sent, hot, pick)
 
 
 def route(tokens, block_split, req_lengths, req_owners):
@@ -250,13 +463,12 @@
     q_row = row // 4 % each
     source = (q_row * count + via_row) * 4 + row % 4
     sent = pick(source[:, None] == row[None, :], tokens)
-    held = lax.all_to_all(sent, "blk", 0, 0, tiled=True)
     row_goal = jnp.repeat(out_spot, 4) * 4 + row % 4
     slots = jnp.arange(count * room * 4, dtype=jnp.int32)
-    sent = pick(slots[:, None] == row_goal[None, :], held)
-    held = lax.all_to_all(sent, "blk", 0, 0, tiled=True)
+    hot = (slots[:, None] == row_goal[None, :]).astype(jnp.bfloat16)
     row_from = jnp.tile(in_spot, 4) * 4 + row // groups
-    return pick(row_from[:, None] == slots[None, :], held), request
+    chosen_rows = (row_from[:, None] == slots[None, :]).astype(jnp.bfloat16)
+    return route_rows(sent, hot, chosen_rows, 4), request
 
 
 def body(
@@ -274,7 +486,6 @@
     merge_weight,
 ):
     rows, width = tokens.shape
-    groups = rows // 4
     routed, request = route(tokens, block_split, req_lengths, req_owners)
     normed1, rest = gather_norm(routed, norm1_gain, 1)
     projected = jnp.einsum(
@@ -296,20 +507,8 @@
     attended = (mixed / jnp.transpose(totals)[:, :, None]).reshape(rows, width).astype(jnp.bfloat16)
     part = jnp.dot(attended, out_weight, preferred_element_type=jnp.float32).astype(jnp.bfloat16)
     normed2, rest = sum_norm(part, rest, norm2_gain, 2)
-    hidden = jax.nn.gelu(
-        jnp.dot(normed2, up_weight, preferred_element_type=jnp.float32), approximate=False
-    ).astype(jnp.bfloat16)
-    part = jnp.dot(hidden, down_weight, preferred_element_type=jnp.float32).astype(jnp.bfloat16)
-    final, unused = sum_norm(part, rest, merge_gain, 3)
-    full = final.shape[1]
-    merged = jnp.zeros((groups, merge_weight.shape[1]), jnp.float32)
-    for k in range(4):
-        merged = merged + jnp.dot(
-            final[k * groups : (k + 1) * groups],
-            merge_weight[k * full : (k + 1) * full],
-            preferred_element_type=jnp.float32,
-        )
-    return merged.astype(jnp.bfloat16)
+    part = mlp(normed2, up_weight, down_weight)
+    return sum_merge(part, rest, merge_gain, merge_weight.T, 3)
 
 
 def solution(mesh):

time: 154 us -> 126 us (0.82)
  the two profiles are of different devices: /device:TPU:0 before, /device:TPU:29 now
where the time goes in v2:
time: 126 us
  Pallas kernels  111 us (88%)
  matrix products  7.56 us (6%)
  other arithmetic  5.71 us (5%)
  local copies, waits for them, and re-layouts  1.32 us (1%)
    pallas_call x1, Pallas kernels, route_rows(): pl.pallas_call(route_kernel, out_shape=jax.ShapeDtypeStruct(sent.shape, j...  34.7 us
    pallas_call x1, Pallas kernels, sum_merge(): pl.pallas_call(sum_merge_kernel, out_shape=jax.ShapeDtypeStruct((rows //...  24.9 us
    pallas_call x1, Pallas kernels, sum_norm(): pl.pallas_call(sum_kernel, out_shape=(jax.ShapeDtypeStruct((rows, full),...  24.1 us
    pallas_call x1, Pallas kernels, gather_norm(): pl.pallas_call(gather_kernel, out_shape=(jax.ShapeDtypeStruct((rows, full...  16.3 us
    pallas_call x1, Pallas kernels, mlp(): pl.pallas_call(mlp_kernel, grid=(steps + 1,), out_shape=jax.ShapeDtypeStr...  11.1 us
    dot_general x1, matrix products, body(): jnp.einsum('td,dcf->ctf', normed1, qkv_weight, preferred_element_type=jnp...  2.53 us

profile of v2, /device:TPU:29, one launch (start us, length us, event | category | flops | bytes accessed | tf_op | source)
XLA Modules:
  0.0 126.0 jit_solution(17035737661612928948)
XLA Ops:
  0.0 0.0 copy-start
  0.0 0.0 copy-start.1
  0.0 1.7 %convolution_convert_fusion.1 = bf16[512,416]{0,1:T(8,128)(2,1)S(1)} fusion(bf16[512,416]{0,1:T(8,128)(2,1)} %param.12, s32[512]{0:T(512)S(1)} %fusion.38), kind=kOutput, calls=%fused_computation.17 | convolution fusion | flops 218578944 | bytes 854016 | tf_op jit(solution)/shard_map/dot_general | solution.py:457
  1.7 0.2 copy.22.sent_ref
  1.9 0.9 select_reduce_fusion.3
  2.8 0.7 fusion.55
  3.5 0.7 broadcast_compare_fusion.1
  4.1 0.7 add_subtract_fusion
  4.8 0.7 select_reduce_fusion.5
  5.6 0.1 select_reduce_fusion
  5.7 0.2 convert_reduce_fusion.1
  5.9 0.1 broadcast_in_dim.72
  6.0 0.1 mul.130
  6.1 0.0 copy-start.4
  6.1 0.2 fusion.17.hot_ref
  6.4 0.2 convert_reduce_fusion
  6.6 0.2 fusion.18.pick_ref
  6.7 34.7 %route_rows.1.x_ref = bf16[512,416]{1,0:T(8,128)(2,1)S(1)} custom-call(bf16[512,416]{1,0:T(8,128)(2,1)S(1)} %copy.22.sent_ref, bf16[640,512]{1,0:T(8,128)(2,1)S(1)} %fusion.17.hot_ref, bf16[512,640]{1,0:T(8,128)(2,1)S(1)} %fusion.18.pick_ref), custom_call_target="tpu_custom_call" | custom-call | tf_op jit(solution)/shard_map/route_rows/pallas_call | solution.py:392
  41.4 0.0 copy-done.1
  41.5 16.3 %gather_norm.1 = (bf16[512,1664]{1,0:T(8,128)(2,1)S(1)}, f32[128,1664]{1,0:T(8,128)S(1)}) custom-call(bf16[512,416]{1,0:T(8,128)(2,1)S(1)} %route_rows.1.x_ref, f32[1,1664]{1,0:T(1,128)S(1)} %reshape.315.gain_ref), custom_call_target="tpu_custom_call" | custom-call | tf_op jit(solution)/shard_map/gather_norm/pallas_call | solution.py:306
  57.8 0.0 copy-done.4
  57.8 2.5 %fusion.11 = bf16[3,512,416]{1,2,0:T(8,128)(2,1)S(1)} fusion(bf16[1664,3,416]{0,2,1:T(8,128)(2,1)S(1)} %copy-done.4, bf16[512,1664]{1,0:T(8,128)(2,1)S(1)} %get-tuple-element.9), kind=kOutput, calls=%fused_computation.11 | convolution fusion | flops 2127151104 | bytes 7135232 | tf_op jit(solution)/shard_map/td,dcf->ctf/dot_general | solution.py:491
  60.3 0.1 fusion.56
  60.4 0.2 broadcast_compare_fusion
  60.7 1.0 fusion
  61.6 0.9 fusion.1
  62.5 0.0 slice-start
  62.5 1.2 fusion.22
  63.8 0.0 copy-start.2
  63.8 0.0 copy-done
  63.8 0.0 slice-start.1
  63.8 1.1 convolution_convert_fusion.part_ref
  65.0 0.0 copy-done.2
  65.0 0.0 slice-start.2
  65.0 24.1 %sum_norm.1 = (bf16[512,1664]{1,0:T(8,128)(2,1)S(1)}, f32[128,1664]{1,0:T(8,128)S(1)}) custom-call(bf16[512,1664]{1,0:T(8,128)(2,1)S(1)} %convolution_convert_fusion.part_ref, f32[128,1664]{1,0:T(8,128)S(1)} %get-tuple-element.10.rest_ref, f32[1,1664]{1,0:T(1,128)S(1)} %reshape.316.gain_ref), custom_call_target="tpu_custom_call" | custom-call | tf_op jit(solution)/shard_map/sum_norm/pallas_call | solution.py:328
  89.1 0.0 slice-done
  89.1 0.0 slice-done.1
  89.1 0.0 copy-start.3
  89.2 0.0 slice-start.3
  89.2 11.1 %mlp.1.part_ref = bf16[512,1664]{1,0:T(8,128)(2,1)S(1)} custom-call(bf16[512,1664]{1,0:T(8,128)(2,1)S(1)} %get-tuple-element.11.x_ref, bf16[1664,2048]{1,0:T(8,128)(2,1)S(1)} %bitcast.33, bf16[2048,1664]{1,0:T(8,128)(2,1)} %down_ref.1), custom_call_target="tpu_custom_call" | custom-call | tf_op jit(solution)/shard_map/mlp/pallas_call | solution.py:370
  100.2 0.0 copy-done.3
  100.3 0.0 slice-done.2
  100.3 0.0 slice-done.3
  100.3 24.9 %sum_merge.1 = bf16[128,416]{1,0:T(8,128)(2,1)S(1)} custom-call(bf16[512,1664]{1,0:T(8,128)(2,1)S(1)} %mlp.1.part_ref, f32[128,1664]{1,0:T(8,128)S(1)} %get-tuple-element.12.rest_ref, f32[1,1664]{1,0:T(1,128)S(1)} %reshape.317.gain_ref, bf16[416,6656]{1,0:T(8,128)(2,1)S(1)} %bitcast.36), custom_call_target="tpu_custom_call" | custom-call | tf_op jit(solution)/shard_map/sum_merge/pallas_call | solution.py:348
  125.2 0.8 copy.24
  (15 shorter events, 0.1 us)
Async XLA Ops:
  0.0 63.8 %copy-start = (bf16[416,1664]{1,0:T(8,128)(2,1)S(1)}, bf16[416,1664]{1,0:T(8,128)(2,1)}, u32[]{:S(2)}) copy-start(bf16[416,1664]{1,0:T(8,128)(2,1)} %param.18) | copy-start | bytes 4153348
  0.0 41.4 %copy-start.1 = (f32[1664]{0:T(1024)S(1)}, f32[1664]{0:T(1024)}, u32[]{:S(2)}) copy-start(f32[1664]{0:T(1024)} %param.16) | copy-start | bytes 19972
  6.1 51.7 %copy-start.4 = (bf16[1664,3,416]{0,2,1:T(8,128)(2,1)S(1)}, bf16[1664,3,416]{0,2,1:T(8,128)(2,1)}, u32[]{:S(2)}) copy-start(bf16[1664,3,416]{0,2,1:T(8,128)(2,1)} %param.17) | copy-start | bytes 12460036
  62.5 26.6 %slice-start = ((s8[6815744]{0:T(1024)(128)(4,1)}), s8[4194304]{0:T(1024)(128)(4,1)S(1)}, s32[]{:S(2)}) async-start(s8[6815744]{0:T(1024)(128)(4,1)} %bitcast.32), calls=%async_computation | async-start | bytes 8388608
  63.8 1.2 copy-start.2
  63.8 25.3 %slice-start.1 = ((s8[6815744]{0:T(1024)(128)(4,1)}), s8[2621440]{0:T(1024)(128)(4,1)S(1)}, s32[]{:S(2)}) async-start(s8[6815744]{0:T(1024)(128)(4,1)} %bitcast.32), calls=%async_computation.1 | async-start | bytes 5242880
  65.0 35.3 %slice-start.2 = ((s8[5537792]{0:T(1024)(128)(4,1)}), s8[1343488]{0:T(1024)(128)(4,1)S(1)}, s32[]{:S(2)}) async-start(s8[5537792]{0:T(1024)(128)(4,1)} %bitcast.34), calls=%async_computation.2 | async-start | bytes 2686976
  89.1 11.1 %copy-start.3 = (f32[1664]{0:T(1024)S(1)}, f32[1664]{0:T(1024)}, u32[]{:S(2)}) copy-start(f32[1664]{0:T(1024)} %param.22) | copy-start | bytes 19972
  89.2 11.1 %slice-start.3 = ((s8[5537792]{0:T(1024)(128)(4,1)}), s8[4194304]{0:T(1024)(128)(4,1)S(1)}, s32[]{:S(2)}) async-start(s8[5537792]{0:T(1024)(128)(4,1)} %bitcast.34), calls=%async_computation.3 | async-start | bytes 8388608
